TPU v7x, 32 devices: a whole 2x2x4 slice. The times are simulated.
32 devices in a mesh: dp: 2 (over y), row: 4 (over z), col: 4 (over x, core).
Axes of the slice: x: 2, y: 2, z: 4, core: 2. Of those that a mesh axis runs over, the one named last changes fastest.
Arguments:
- images_in: bfloat16 [8, 64, 64, 1024], P('dp', 'row', 'col'), may hold values from -6 to 6
- keep: int32 [8], P('dp'), may hold values from 0 to 1, as said below
- dw_weight: bfloat16 [49, 1024], replicated, may hold values from -0.875 to 0.875
- layer_norm_gain: float32 [1024], replicated, may hold values from 0.25 to 1.75
- w_in: bfloat16 [1024, 2048], replicated, may hold values from -0.1875 to 0.1875
- w_out: bfloat16 [2048, 1024], replicated, may hold values from -0.125 to 0.125
- layer_scale: float32 [1024], replicated, may hold values from 0.25 to 1
- out_grad: bfloat16 [8, 64, 64, 1024], P('dp', 'row', 'col'), may hold values from -6 to 6
Outputs:
- output: bfloat16 [8, 64, 64, 1024], P('dp', 'row', 'col')
- grad_input: bfloat16 [8, 64, 64, 1024], P('dp', 'row', 'col')
- grad_w_in: float32 [1024, 2048], P(('dp', 'row', 'col'))
- grad_w_out: float32 [2048, 1024], P(('dp', 'row', 'col'))
- grad_dw: float32 [49, 1024], replicated
- grad_ln_gain: float32 [1024], replicated
- grad_layer_scale: float32 [1024], replicated
Inputs may be any that keep to these rules, and one draw needn't show every extreme that they name: `keep`: 1 keeps the image's residual branch, 0 drops it; at least one and at most 4 images are dropped.
All inputs are finite; a program needn't handle non-finite values.
Results may differ from a plain program's by a relative error of at most 0.0062.
Values may be sent and summed in bfloat16 or wider, within the bound.
A program may use at most 128 MiB of HBM per device.

v0:
```python
import math
import jax
import jax.numpy as jnp
from jax import lax
from jax.sharding import PartitionSpec as P

KERNEL = 7
eps = 1e-06
keep_rate = 0.75


def extended(block, sides, width):
    for axis, dim in sides:
        count = lax.axis_size(axis)
        forward = [(i, i + 1) for i in range(count - 1)]
        backward = [(target, source) for source, target in forward]
        low = lax.ppermute(
            lax.slice_in_dim(block, block.shape[dim] - width, None, axis=dim), axis, forward
        )
        high = lax.ppermute(lax.slice_in_dim(block, 0, width, axis=dim), axis, backward)
        block = jnp.concatenate([low, block, high], axis=dim)
    return block


def depthwise(padded, kernel, width):
    taps = kernel.reshape(KERNEL, KERNEL, 1, width)
    return lax.conv_general_dilated(
        padded,
        taps,
        (1, 1),
        "VALID",
        dimension_numbers=("NHWC", "HWIO", "NHWC"),
        feature_group_count=width,
        preferred_element_type=jnp.float32,
    )


def extend(field):
    return extended(field, (("row", 1), ("col", 2)), KERNEL // 2)


def shards(images_in, keep, dw_weight, layer_norm_gain, w_in, w_out, layer_scale, out_grad):
    batch, tile_h, tile_w, width = images_in.shape
    cells = tile_h * tile_w
    total_rows = batch * cells
    padded = extend(images_in)
    conv = depthwise(padded, dw_weight, width).reshape(total_rows, width)
    mean_v = jnp.mean(conv, axis=-1, keepdims=True)
    local_device = conv - mean_v
    inverse_deviation = lax.rsqrt(
        jnp.mean(local_device * local_device, axis=-1, keepdims=True) + eps
    )
    centered_scaled_input = local_device * inverse_deviation
    normalized_input = (centered_scaled_input * layer_norm_gain).astype(jnp.bfloat16)
    pre = jnp.dot(normalized_input, w_in, preferred_element_type=jnp.float32)
    cdf = 0.5 * (1.0 + lax.erf(pre * (1.0 / math.sqrt(2.0))))
    hidden = (pre * cdf).astype(jnp.bfloat16)
    branch = jnp.dot(hidden, w_out, preferred_element_type=jnp.float32)
    factor = jnp.repeat(keep.astype(jnp.float32) / keep_rate, cells)[:, None]
    flat_in = images_in.reshape(total_rows, width).astype(jnp.float32)
    output = (flat_in + factor * layer_scale * branch).astype(jnp.bfloat16).reshape(images_in.shape)
    upstream = out_grad.reshape(total_rows, width).astype(jnp.float32)
    g_branch = (factor * layer_scale * upstream).astype(jnp.bfloat16)
    gamma_term = jnp.sum(factor * upstream * branch, axis=0)
    slope = cdf + pre * jnp.exp(-0.5 * pre * pre) * (1.0 / math.sqrt(2.0 * math.pi))
    g_pre = (jnp.dot(g_branch, w_out.T, preferred_element_type=jnp.float32) * slope).astype(
        jnp.bfloat16
    )
    normalized_gradient = jnp.dot(g_pre, w_in.T, preferred_element_type=jnp.float32)
    gain_contribution = jnp.sum(normalized_gradient * centered_scaled_input, axis=0)
    input_gradient = normalized_gradient * layer_norm_gain
    convolution_gradient = (
        inverse_deviation
        * (
            input_gradient
            - jnp.mean(input_gradient, axis=-1, keepdims=True)
            - centered_scaled_input
            * jnp.mean(input_gradient * centered_scaled_input, axis=-1, keepdims=True)
        )
    ).astype(jnp.bfloat16)
    g_conv4 = convolution_gradient.reshape(batch, tile_h, tile_w, width)
    g_wide = g_conv4.astype(jnp.float32)
    dw_terms = []
    for i in range(KERNEL):
        for j in range(KERNEL):
            window = padded[:, i : i + tile_h, j : j + tile_w, :].astype(jnp.float32)
            dw_terms.append(jnp.sum(g_wide * window, axis=(0, 1, 2)))
    dw_term = jnp.stack(dw_terms, axis=0)
    flipped = dw_weight.reshape(KERNEL, KERNEL, width)[::-1, ::-1].reshape(KERNEL * KERNEL, width)
    back = depthwise(extend(g_conv4), flipped, width).reshape(total_rows, width)
    grad_input = (upstream + back).astype(jnp.bfloat16).reshape(images_in.shape)
    images = jnp.float32(batch * lax.axis_size("dp"))
    dw_sum, gain_sum, gamma_sum = lax.psum(
        (dw_term, gain_contribution, gamma_term), ("dp", "row", "col")
    )
    w_in_term = jnp.dot(normalized_input.T, g_pre, preferred_element_type=jnp.float32)
    w_out_term = jnp.dot(hidden.T, g_branch, preferred_element_type=jnp.float32)
    w_in_sum, w_out_sum = (
        lax.psum_scatter(w_in_term, ("dp", "row", "col"), scatter_dimension=0, tiled=True),
        lax.psum_scatter(w_out_term, ("dp", "row", "col"), scatter_dimension=0, tiled=True),
    )
    return (
        output,
        grad_input,
        w_in_sum / images,
        w_out_sum / images,
        dw_sum / images,
        gain_sum / images,
        gamma_sum / images,
    )


def solution(mesh):
    placed = (
        P("dp", "row", "col", None),
        P("dp"),
        P(),
        P(),
        P(),
        P(),
        P(),
        P("dp", "row", "col", None),
    )
    return jax.shard_map(
        shards,
        mesh=mesh,
        in_specs=placed,
        out_specs=(
            P("dp", "row", "col", None),
            P("dp", "row", "col", None),
            P(("dp", "row", "col"), None),
            P(("dp", "row", "col"), None),
            P(),
            P(),
            P(),
        ),
        check_vma=False,
    )
```

profile of v0, /device:TPU:0, one launch (start us, length us, event | category | flops | bytes accessed | tf_op | source)
XLA Modules:
  0.0 644.9 jit_solution(5006209415736164986)
XLA Ops:
  7.2 1.3 fusion.121
  8.9 5.0 collective-permute-start
  14.2 1.3 collective-permute-start.1
  15.5 6.7 %collective-permute-done = bf16[4,3,16,1024]{3,0,2,1:T(4,128)(2,1)S(1)} collective-permute-done((bf16[4,3,16,1024]{3,0,2,1:T(4,128)(2,1)S(1)}, bf16[4,3,16,1024]{3,0,2,1:T(4,128)(2,1)S(1)}, u32[]{:S(2)}, u32[]{:S(2)}) %collective-permute-start) | collective-permute-done | bytes 393248 | tf_op jit(solution)/shard_map/ppermute | solution.py:17
  22.5 4.3 constant_dynamic-update-slice_fusion.6
  27.1 1.4 copy-done.3
  29.2 1.4 fusion.119
  30.6 2.2 collective-permute-start.2
  34.1 4.2 copy_convert_fusion
  39.1 6.7 %copy.73 = f32[4,16,16,1024]{3,2,1,0:T(8,128)} copy(f32[4,16,16,1024]{3,0,2,1:T(4,128)} %copy_convert_fusion) | data formatting | bytes 8388608 | tf_op jit(solution)/shard_map/convert_element_type | solution.py:62
  46.5 4.4 copy.63
  50.9 25.2 %fusion.122 = (f32[4,16,16]{0,2,1:T(8,128)S(1)}, f32[4,16,16,1024]{3,0,2,1:T(4,128)}) fusion(bf16[7,7,1,1024]{3,2,1,0:T(2,128)(2,1)S(1)} %copy-done.19, bf16[4,22,3,1024]{3,0,2,1:T(4,128)(2,1)S(1)} %collective-permute-done.3, bf16[4,22,16,1024]{3,0,2,1:T(4,128)(2,1)S(1)} %get-tuple-element.113, bf16[4,22,3,1024]{3,0,2,1:T(4,128)(2,1)} %collective-permute-done.2), kind=kOutput, calls=%fused_computation.248 | convolution fusion | flops 115702784 | bytes 8263680 | tf_op jit(solution)/shard_map/conv_general_dilated | solution.py:27
  76.6 6.7 %copy.68 = f32[4,16,16,1024]{3,2,1,0:T(8,128)} copy(f32[4,16,16,1024]{3,0,2,1:T(4,128)} %get-tuple-element.115) | data formatting | bytes 8388608 | tf_op jit(solution)/shard_map/conv_general_dilated | solution.py:27
  83.3 1.4 multiply_reduce_fusion.2
  84.9 2.9 multiply_convert_fusion.2
  88.4 7.0 %multiply_convert_fusion = (bf16[1024,2048]{1,0:T(8,128)(2,1)S(1)}, f32[1024,2048]{1,0:T(8,128)}) fusion(bf16[1024,1024]{1,0:T(8,128)(2,1)S(1)} %multiply_convert_fusion.2, bf16[1024,2048]{1,0:T(8,128)(2,1)S(1)} %copy-done.23), kind=kOutput, calls=%fused_computation.96 | convolution fusion | flops 4305453056 | bytes 18874368 | tf_op jit(solution)/shard_map/dot_general | solution.py:55
  95.4 2.4 copy-done.22
  97.8 6.8 %fusion.59 = (f32[1024]{0:T(1024)S(1)}, bf16[1024,1024]{1,0:T(8,128)(2,1)S(1)}, bf16[1024,1024]{1,0:T(8,128)(2,1)}) fusion(f32[4,16,16,1024]{3,2,1,0:T(8,128)S(1)} %copy-done.11, f32[1024]{0:T(1024)S(1)} %bitcast.150, f32[1024]{0:T(1024)S(1)} %copy-done.24, f32[4,16,16,1024]{3,2,1,0:T(8,128)S(1)} %copy-done.12, ...), kind=kOutput, calls=%fused_computation.154 | convolution fusion | flops 4304403456 | bytes 20983808 | tf_op jit(solution)/shard_map/dot_general | solution.py:58
  104.6 9.9 %fusion.5 = bf16[1024,2048]{1,0:T(8,128)(2,1)S(1)} fusion(f32[1024,2048]{1,0:T(8,128)} %get-tuple-element.117, bf16[1024,1024]{1,0:T(8,128)(2,1)S(1)} %get-tuple-element.96, bf16[2048,1024]{1,0:T(8,128)(2,1)S(1)} %copy-done.22), kind=kOutput, calls=%fused_computation.95 | convolution fusion | flops 4315938816 | bytes 18874368 | tf_op jit(solution)/shard_map/dot_general | solution.py:66
  114.6 5.1 multiply_reduce_fusion
  119.8 1.7 multiply_convert_fusion.1
  122.2 8.2 %fusion.54 = (f32[1024]{0:T(1024)S(1)}, f32[1024]{0:T(1024)S(1)}, f32[1024]{0:T(1024)S(1)}, f32[1024]{0:T(1024)S(1)}, f32[1024]{0:T(1024)S(1)}, /*index=5*/f32[1024]{0:T(1024)S(1)}) fusion(bf16[4,19,16,1024]{3,0,2,1:T(4,128)(2,1)S(1)} %copy-done.4, bf16[4,16,16,1024]{3,2,1,0:T(8,128)(2,1)S(1)} %bitcast.90, bf16[4,19,16,1024]{3,0,2,1:T(4,128)(2,1)S(1)} %copy-done.6), kind=kLoop, calls=%fused_computation.148 | loop fusion | flops 19916800 | bytes 14704640 | tf_op jit(solution)/shard_map/reduce_sum | solution.py:87
  130.4 10.7 %fusion.50 = (f32[1024]{0:T(1024)S(1)}, f32[1024]{0:T(1024)S(1)}, f32[1024]{0:T(1024)S(1)}, f32[1024]{0:T(1024)S(1)}, f32[1024]{0:T(1024)S(1)}, /*index=5*/f32[1024]{0:T(1024)S(1)}) fusion(bf16[4,22,3,1024]{3,0,2,1:T(4,128)(2,1)S(1)} %collective-permute-done.3, bf16[4,22,16,1024]{3,0,2,1:T(4,128)(2,1)S(1)} %copy-done.1, ...), kind=kLoop, calls=%fused_computation.144 | loop fusion | flops 26208256 | bytes 6086656 | tf_op jit(solution)/shard_map/reduce_sum | solution.py:87
  141.1 9.7 %fusion.55 = (f32[1024]{0:T(1024)S(1)}, f32[1024]{0:T(1024)S(1)}, f32[1024]{0:T(1024)S(1)}, f32[1024]{0:T(1024)S(1)}, f32[1024]{0:T(1024)S(1)}, /*index=5*/f32[1024]{0:T(1024)S(1)}) fusion(bf16[4,22,3,1024]{3,0,2,1:T(4,128)(2,1)S(1)} %collective-permute-done.3, bf16[4,22,16,1024]{3,0,2,1:T(4,128)(2,1)S(1)} %copy-done.1, ...), kind=kLoop, calls=%fused_computation.149 | loop fusion | flops 26208256 | bytes 5545984 | tf_op jit(solution)/shard_map/reduce_sum | solution.py:87
  150.8 10.8 %fusion.51 = (f32[1024]{0:T(1024)S(1)}, f32[1024]{0:T(1024)S(1)}, f32[1024]{0:T(1024)S(1)}, f32[1024]{0:T(1024)S(1)}, f32[1024]{0:T(1024)S(1)}, /*index=5*/f32[1024]{0:T(1024)S(1)}) fusion(bf16[4,22,3,1024]{3,0,2,1:T(4,128)(2,1)} %collective-permute-done.2, bf16[4,22,16,1024]{3,0,2,1:T(4,128)(2,1)S(1)} %copy-done.1, bf16[4,16,16,1024]{3,2,1,0:T(8,128)(2,1)S(1)} %bitcast.93), kind=kLoop, calls=%fused_computation.145 | loop fusion | flops 26208256 | bytes 5545984 | tf_op jit(solution)/shard_map/reduce_sum | solution.py:87
  161.6 10.3 %fusion.56 = (f32[1024]{0:T(1024)S(1)}, f32[1024]{0:T(1024)S(1)}, f32[1024]{0:T(1024)S(1)}, f32[1024]{0:T(1024)S(1)}, f32[1024]{0:T(1024)S(1)}, /*index=5*/f32[1024]{0:T(1024)S(1)}) fusion(bf16[4,22,3,1024]{3,0,2,1:T(4,128)(2,1)S(1)} %collective-permute-done.3, bf16[4,22,16,1024]{3,0,2,1:T(4,128)(2,1)S(1)} %copy-done.1, ...), kind=kLoop, calls=%fused_computation.150 | loop fusion | flops 26208256 | bytes 5545984 | tf_op jit(solution)/shard_map/reduce_sum | solution.py:87
  171.9 10.9 %fusion.52 = (f32[1024]{0:T(1024)S(1)}, f32[1024]{0:T(1024)S(1)}, f32[1024]{0:T(1024)S(1)}, f32[1024]{0:T(1024)S(1)}, f32[1024]{0:T(1024)S(1)}, /*index=5*/f32[1024]{0:T(1024)S(1)}) fusion(bf16[4,22,3,1024]{3,0,2,1:T(4,128)(2,1)} %collective-permute-done.2, bf16[4,22,16,1024]{3,0,2,1:T(4,128)(2,1)S(1)} %copy-done.1, bf16[4,16,16,1024]{3,2,1,0:T(8,128)(2,1)S(1)} %bitcast.95), kind=kLoop, calls=%fused_computation.146 | loop fusion | flops 26208256 | bytes 5545984 | tf_op jit(solution)/shard_map/reduce_sum | solution.py:87
  182.8 11.6 %fusion.57 = (f32[1024]{0:T(1024)S(1)}, f32[1024]{0:T(1024)S(1)}, f32[1024]{0:T(1024)S(1)}, f32[1024]{0:T(1024)S(1)}, f32[1024]{0:T(1024)S(1)}, /*index=5*/f32[1024]{0:T(1024)S(1)}, f32[1024]{0:T(1024)S(1)}) fusion(bf16[4,22,3,1024]{3,0,2,1:T(4,128)(2,1)S(1)} %collective-permute-done.3, bf16[4,22,16,1024]{3,0,2,1:T(4,128)(2,1)S(1)} %copy-done.1, ...), kind=kLoop, calls=%fused_computation.151 | loop fusion | flops 29352960 | bytes 7647232 | tf_op jit(solution)/shard_map/reduce_sum | solution.py:87
  194.4 10.8 %fusion.53 = (f32[1024]{0:T(1024)S(1)}, f32[1024]{0:T(1024)S(1)}, f32[1024]{0:T(1024)S(1)}, f32[1024]{0:T(1024)S(1)}, f32[1024]{0:T(1024)S(1)}, /*index=5*/f32[1024]{0:T(1024)S(1)}) fusion(bf16[4,22,16,1024]{3,0,2,1:T(4,128)(2,1)S(1)} %copy-done.1, bf16[4,22,3,1024]{3,0,2,1:T(4,128)(2,1)} %collective-permute-done.2, bf16[4,16,16,1024]{3,2,1,0:T(8,128)(2,1)S(1)} %bitcast.97), kind=kLoop, calls=%fused_computation.147 | loop fusion | flops 26208256 | bytes 5545984 | tf_op jit(solution)/shard_map/reduce_sum | solution.py:87
  205.2 4.6 stack.199
  209.9 10.7 %fusion.124 = f32[2048,1024]{1,0:T(8,128)} fusion(bf16[1024,2048]{1,0:T(8,128)(2,1)} %copy-done.27, bf16[1024,1024]{1,0:T(8,128)(2,1)} %copy-done.28), kind=kOutput, calls=%fused_computation.250 | convolution fusion | flops 4294967296 | bytes 14680064 | tf_op jit(solution)/shard_map/dot_general | solution.py:97
  220.8 10.6 %fusion.123 = f32[1024,2048]{1,0:T(8,128)} fusion(bf16[1024,1024]{1,0:T(8,128)(2,1)} %copy-done.15, bf16[1024,2048]{1,0:T(8,128)(2,1)} %copy-done.26), kind=kOutput, calls=%fused_computation.249 | convolution fusion | flops 4294967296 | bytes 14680064 | tf_op jit(solution)/shard_map/dot_general | solution.py:96
  231.8 4.4 collective-permute-start.4
  236.6 1.3 collective-permute-start.5
  237.9 6.9 %collective-permute-done.4 = bf16[4,3,16,1024]{3,0,2,1:T(4,128)(2,1)S(1)} collective-permute-done((bf16[4,3,16,1024]{3,0,2,1:T(4,128)(2,1)S(1)}, bf16[4,3,16,1024]{3,0,2,1:T(4,128)(2,1)S(1)}, u32[]{:S(2)}, u32[]{:S(2)}) %collective-permute-start.4) | collective-permute-done | bytes 393248 | tf_op jit(solution)/shard_map/ppermute | solution.py:17
  244.9 1.9 constant_dynamic-update-slice_fusion.4
  246.8 2.8 collective-permute-done.5
  249.8 1.6 copy-done.16
  251.8 3.4 collective-permute-start.6
  257.0 43.0 %all-reduce = (f32[1024]{0:T(1024)S(1)}, f32[1024]{0:T(1024)S(1)}) all-reduce(f32[1024]{0:T(1024)S(1)} %get-tuple-element.35, f32[1024]{0:T(1024)S(1)} %get-tuple-element.95), channel_id=1, replica_groups=mesh['dp'=2,'row'=4,'col'=4] {'dp','row','col'}, use_global_device_ids=true, to_apply=%region_57.0 | all-reduce | flops 2048 | bytes 16384 | tf_op jit(solution)/shard_map/psum | solution.py:93
  300.5 37.1 %all-reduce.3.cloned.1.call-done = f32[49,1024]{1,0:T(8,128)} async-done(((f32[49,1024]{1,0:T(8,128)}), f32[49,1024]{1,0:T(8,128)}) %all-reduce.3.cloned.1.call-update) | async-done | bytes 200720 | tf_op jit(solution)/shard_map/psum | solution.py:93
  337.6 1.6 broadcast_multiply_fusion.2
  339.3 24.3 %add_convert_fusion = bf16[4,16,16,1024]{3,0,2,1:T(4,128)(2,1)S(1)} fusion(bf16[4,22,3,1024]{3,0,2,1:T(4,128)(2,1)} %collective-permute-done.7, bf16[4,22,16,1024]{3,0,2,1:T(4,128)(2,1)} %copy-done.16, bf16[4,22,3,1024]{3,0,2,1:T(4,128)(2,1)} %collective-permute-done.6, bf16[4,16,16,1024]{3,2,1,0:T(8,128)(2,1)S(1)} %copy-done.14, ...), kind=kOutput, calls=%fused_computation.158 | convolution fusion | flops 117800960 | bytes 8259584 | tf_op jit(solution)/shard_map/conv_general_dilated | solution.py:27
  363.5 1.9 copy.81
  365.5 123.5 %reduce-scatter.5.cloned.1.call-done = f32[64,1024]{1,0:T(8,128)} async-done(((f32[2048,1024]{1,0:T(8,128)}), f32[64,1024]{1,0:T(8,128)}) %reduce-scatter.5.cloned.1.call-update) | async-done | bytes 262160 | tf_op jit(solution)/shard_map/reduce_scatter | solution.py:100
  489.0 1.7 broadcast_multiply_fusion
  490.7 145.8 %reduce-scatter.3.cloned.1.call-done = f32[32,2048]{1,0:T(8,128)} async-done(((f32[1024,2048]{1,0:T(8,128)}), f32[32,2048]{1,0:T(8,128)}) %reduce-scatter.3.cloned.1.call-update) | async-done | bytes 262160 | tf_op jit(solution)/shard_map/reduce_scatter | solution.py:99
  636.4 1.7 broadcast_multiply_fusion.1
  (93 shorter events, 10.7 us)
Async XLA Ops:
  7.2 330.4 %all-reduce.3.cloned.1.call-start = ((), (), s32[]{:S(2)}) async-start(), calls=%async_computation.4 | async-start | bytes 458752 | tf_op jit(solution)/shard_map/psum | solution.py:93
  7.2 15.3 %copy-start.9 = (bf16[4,16,16,1024]{3,2,1,0:T(8,128)(2,1)S(1)}, bf16[4,16,16,1024]{3,2,1,0:T(8,128)(2,1)}, u32[]{:S(2)}) copy-start(bf16[4,16,16,1024]{3,2,1,0:T(8,128)(2,1)} %param.8) | copy-start | bytes 6291460
  8.9 13.3 %collective-permute-start = (bf16[4,3,16,1024]{3,0,2,1:T(4,128)(2,1)S(1)}, bf16[4,3,16,1024]{3,0,2,1:T(4,128)(2,1)S(1)}, u32[]{:S(2)}, u32[]{:S(2)}) collective-permute-start(bf16[4,3,16,1024]{3,0,2,1:T(4,128)(2,1)S(1)} %copy.143), channel_id=1, source_target_pairs={{0,4},{4,8},{8,12},{1,5},{5,9},{9,13},{2,6},{6,10},{10,14},{3,7},{... | collective-permute-start | bytes 1179656 | tf_op jit(solution)/shard_map/ppermute | solution.py:17
  14.2 12.6 %collective-permute-start.1 = (bf16[4,3,16,1024]{3,0,2,1:T(4,128)(2,1)S(1)}, bf16[4,3,16,1024]{3,0,2,1:T(4,128)(2,1)S(1)}, u32[]{:S(2)}, u32[]{:S(2)}) collective-permute-start(bf16[4,3,16,1024]{3,0,2,1:T(4,128)(2,1)S(1)} %copy.144), channel_id=1, source_target_pairs={{4,0},{8,4},{12,8},{5,1},{9,5},{13,9},{6,2},{10,6},{14,10},{7,3},{... | collective-permute-start | bytes 1179656 | tf_op jit(solution)/shard_map/ppermute | solution.py:20
  26.7 2.4 copy-start.5
  26.7 7.3 %copy-start.13 = (bf16[4,16,16,1024]{3,2,1,0:T(8,128)(2,1)S(1)}, bf16[4,16,16,1024]{3,2,1,0:T(8,128)(2,1)}, u32[]{:S(2)}) copy-start(bf16[4,16,16,1024]{3,2,1,0:T(8,128)(2,1)} %param.15) | copy-start | bytes 6291460
  27.1 1.5 copy-start.3
  28.6 22.4 %copy-start = (bf16[4,22,16,1024]{3,0,2,1:T(4,128)(2,1)}, bf16[4,22,16,1024]{3,0,2,1:T(4,128)(2,1)S(1)}, u32[]{:S(2)}) copy-start(bf16[4,22,16,1024]{3,0,2,1:T(4,128)(2,1)S(1)} %get-tuple-element.113) | copy-start | bytes 8650756
  30.6 7.8 %copy-start.17 = (bf16[49,1024]{1,0:T(8,128)(2,1)S(1)}, bf16[49,1024]{1,0:T(8,128)(2,1)}, u32[]{:S(2)}) copy-start(bf16[49,1024]{1,0:T(8,128)(2,1)} %param.10) | copy-start | bytes 301060
  30.6 20.3 %collective-permute-start.2 = (bf16[4,22,3,1024]{3,0,2,1:T(4,128)(2,1)}, bf16[4,22,3,1024]{3,0,2,1:T(4,128)(2,1)}, u32[]{:S(2)}, u32[]{:S(2)}) collective-permute-start(bf16[4,22,3,1024]{3,0,2,1:T(4,128)(2,1)} %get-tuple-element.100), channel_id=1, source_target_pairs={{0,1},{1,2},{2,3},{4,5},{5,6},{6,7},{8,9},{9,10},{10,11},{12,13},{... | collective-permute-start | bytes 1622024 | tf_op jit(solution)/shard_map/ppermute | solution.py:17
  32.8 18.1 %collective-permute-start.3 = (bf16[4,22,3,1024]{3,0,2,1:T(4,128)(2,1)}, bf16[4,22,3,1024]{3,0,2,1:T(4,128)(2,1)S(1)}, u32[]{:S(2)}, u32[]{:S(2)}) collective-permute-start(bf16[4,22,3,1024]{3,0,2,1:T(4,128)(2,1)} %get-tuple-element.101), channel_id=1, source_target_pairs={{1,0},{2,1},{3,2},{5,4},{6,5},{7,6},{9,8},{10,9},{11,10},{13,12},{... | collective-permute-start | bytes 1622024 | tf_op jit(solution)/shard_map/ppermute | solution.py:20
  39.1 6.7 %copy-start.25 = (s32[4]{0:T(128)S(1)}, s32[4]{0:T(128)}, u32[]{:S(2)}) copy-start(s32[4]{0:T(128)} %param.9) | copy-start | bytes 52
  39.1 7.4 %copy-start.7 = (f32[4,16,16,1024]{3,0,2,1:T(4,128)S(1)}, f32[4,16,16,1024]{3,0,2,1:T(4,128)}, u32[]{:S(2)}) copy-start(f32[4,16,16,1024]{3,0,2,1:T(4,128)} %get-tuple-element.103) | copy-start | bytes 12582916
  46.5 4.4 copy-start.19
  76.6 6.7 %copy-start.8 = (f32[4,16,16,1024]{3,0,2,1:T(4,128)S(1)}, f32[4,16,16,1024]{3,0,2,1:T(4,128)}, u32[]{:S(2)}) copy-start(f32[4,16,16,1024]{3,0,2,1:T(4,128)} %get-tuple-element.115) | copy-start | bytes 12582916
  83.3 1.7 copy-start.20
  84.9 3.5 copy-start.23
  88.4 7.0 %copy-start.15 = (bf16[1024,1024]{1,0:T(8,128)(2,1)}, bf16[1024,1024]{1,0:T(8,128)(2,1)S(1)}, u32[]{:S(2)}) copy-start(bf16[1024,1024]{1,0:T(8,128)(2,1)S(1)} %multiply_convert_fusion.2) | copy-start | bytes 6291460
  88.4 7.0 %copy-start.11 = (f32[4,16,16,1024]{3,2,1,0:T(8,128)S(1)}, f32[4,16,16,1024]{3,2,1,0:T(8,128)}, u32[]{:S(2)}) copy-start(f32[4,16,16,1024]{3,2,1,0:T(8,128)} %copy.73) | copy-start | bytes 12582916
  88.4 7.0 %copy-start.12 = (f32[4,16,16,1024]{3,2,1,0:T(8,128)S(1)}, f32[4,16,16,1024]{3,2,1,0:T(8,128)}, u32[]{:S(2)}) copy-start(f32[4,16,16,1024]{3,2,1,0:T(8,128)} %copy.63) | copy-start | bytes 12582916
  88.4 7.0 %copy-start.21 = (f32[1,2,4,128]{3,1,2,0:T(2,128)S(1)}, f32[1,2,4,128]{3,1,2,0:T(2,128)}, u32[]{:S(2)}) copy-start(f32[1,2,4,128]{3,1,2,0:T(2,128)} %copy.82) | copy-start | bytes 12292
  88.4 9.4 %copy-start.22 = (bf16[2048,1024]{1,0:T(8,128)(2,1)S(1)}, bf16[2048,1024]{1,0:T(8,128)(2,1)}, u32[]{:S(2)}) copy-start(bf16[2048,1024]{1,0:T(8,128)(2,1)} %param.13) | copy-start | bytes 12582916
  88.4 9.4 %copy-start.24 = (f32[1024]{0:T(1024)S(1)}, f32[1024]{0:T(1024)}, u32[]{:S(2)}) copy-start(f32[1024]{0:T(1024)} %param.14) | copy-start | bytes 12292
  95.4 9.2 %copy-start.27 = (bf16[1024,2048]{1,0:T(8,128)(2,1)}, bf16[1024,2048]{1,0:T(8,128)(2,1)S(1)}, u32[]{:S(2)}) copy-start(bf16[1024,2048]{1,0:T(8,128)(2,1)S(1)} %get-tuple-element.116) | copy-start | bytes 12582916
  104.6 10.0 %copy-start.28 = (bf16[1024,1024]{1,0:T(8,128)(2,1)}, bf16[1024,1024]{1,0:T(8,128)(2,1)S(1)}, u32[]{:S(2)}) copy-start(bf16[1024,1024]{1,0:T(8,128)(2,1)S(1)} %get-tuple-element.96) | copy-start | bytes 6291460
  104.6 10.0 %copy-start.2 = (f32[4,16,16,1024]{3,2,1,0:T(8,128)S(1)}, f32[4,16,16,1024]{3,2,1,0:T(8,128)}, u32[]{:S(2)}) copy-start(f32[4,16,16,1024]{3,2,1,0:T(8,128)} %copy.68) | copy-start | bytes 12582916
  114.6 5.1 copy-start.26
  119.7 1.7 copy-start.4
  119.8 2.4 copy-start.6
  122.2 8.2 %copy-start.1 = (bf16[4,22,16,1024]{3,0,2,1:T(4,128)(2,1)S(1)}, bf16[4,22,16,1024]{3,0,2,1:T(4,128)(2,1)}, u32[]{:S(2)}) copy-start(bf16[4,22,16,1024]{3,0,2,1:T(4,128)(2,1)} %copy-done) | copy-start | bytes 8650756
  171.9 10.9 %copy-start.10 = (bf16[4,16,16,1024]{3,2,1,0:T(8,128)(2,1)S(1)}, bf16[4,16,16,1024]{3,2,1,0:T(8,128)(2,1)}, u32[]{:S(2)}) copy-start(bf16[4,16,16,1024]{3,2,1,0:T(8,128)(2,1)} %param.8) | copy-start | bytes 6291460
  209.9 279.1 %reduce-scatter.5.cloned.1.call-start = ((), (), s32[]{:S(2)}) async-start(), calls=%async_computation.3 | async-start | bytes 8650752 | tf_op jit(solution)/shard_map/reduce_scatter | solution.py:100
  220.6 415.8 %reduce-scatter.3.cloned.1.call-start = ((), (), s32[]{:S(2)}) async-start(), calls=%async_computation.2 | async-start | bytes 8650752 | tf_op jit(solution)/shard_map/reduce_scatter | solution.py:99
  231.8 13.0 %collective-permute-start.4 = (bf16[4,3,16,1024]{3,0,2,1:T(4,128)(2,1)S(1)}, bf16[4,3,16,1024]{3,0,2,1:T(4,128)(2,1)S(1)}, u32[]{:S(2)}, u32[]{:S(2)}) collective-permute-start(bf16[4,3,16,1024]{3,0,2,1:T(4,128)(2,1)S(1)} %copy.145), channel_id=1, source_target_pairs={{0,4},{4,8},{8,12},{1,5},{5,9},{9,13},{2,6},{6,10},{10,14},{3,7},{... | collective-permute-start | bytes 1179656 | tf_op jit(solution)/shard_map/ppermute | solution.py:17
  236.6 13.1 %collective-permute-start.5 = (bf16[4,3,16,1024]{3,0,2,1:T(4,128)(2,1)S(1)}, bf16[4,3,16,1024]{3,0,2,1:T(4,128)(2,1)S(1)}, u32[]{:S(2)}, u32[]{:S(2)}) collective-permute-start(bf16[4,3,16,1024]{3,0,2,1:T(4,128)(2,1)S(1)} %copy.146), channel_id=1, source_target_pairs={{4,0},{8,4},{12,8},{5,1},{9,5},{13,9},{6,2},{10,6},{14,10},{7,3},{... | collective-permute-start | bytes 1179656 | tf_op jit(solution)/shard_map/ppermute | solution.py:20
  244.9 11.6 %copy-start.18 = (bf16[49,1024]{1,0:T(8,128)(2,1)S(1)}, bf16[49,1024]{1,0:T(8,128)(2,1)}, u32[]{:S(2)}) copy-start(bf16[49,1024]{1,0:T(8,128)(2,1)} %param.10) | copy-start | bytes 301060
  246.8 92.4 %copy-start.14 = (bf16[4,16,16,1024]{3,2,1,0:T(8,128)(2,1)S(1)}, bf16[4,16,16,1024]{3,2,1,0:T(8,128)(2,1)}, u32[]{:S(2)}) copy-start(bf16[4,16,16,1024]{3,2,1,0:T(8,128)(2,1)} %param.15) | copy-start | bytes 6291460
  249.8 1.6 copy-start.16
  251.8 87.4 %collective-permute-start.6 = (bf16[4,22,3,1024]{3,0,2,1:T(4,128)(2,1)S(1)}, bf16[4,22,3,1024]{3,0,2,1:T(4,128)(2,1)}, u32[]{:S(2)}, u32[]{:S(2)}) collective-permute-start(bf16[4,22,3,1024]{3,0,2,1:T(4,128)(2,1)S(1)} %get-tuple-element.98), channel_id=1, source_target_pairs={{0,1},{1,2},{2,3},{4,5},{5,6},{6,7},{8,9},{9,10},{10,11},{12,13},{... | collective-permute-start | bytes 1622024 | tf_op jit(solution)/shard_map/ppermute | solution.py:17
  255.2 84.0 %collective-permute-start.7 = (bf16[4,22,3,1024]{3,0,2,1:T(4,128)(2,1)S(1)}, bf16[4,22,3,1024]{3,0,2,1:T(4,128)(2,1)}, u32[]{:S(2)}, u32[]{:S(2)}) collective-permute-start(bf16[4,22,3,1024]{3,0,2,1:T(4,128)(2,1)S(1)} %get-tuple-element.99), channel_id=1, source_target_pairs={{1,0},{2,1},{3,2},{5,4},{6,5},{7,6},{9,8},{10,9},{11,10},{13,12},{... | collective-permute-start | bytes 1622024 | tf_op jit(solution)/shard_map/ppermute | solution.py:20
Sparse Core Ops, SparseCore 0:
  210.0 127.5 all-reduce.2
  339.9 149.0 reduce-scatter.4
  491.3 145.0 reduce-scatter.2
where the time goes:
time: 653 us; the launch traced here: 645 us
  waiting for transfers between devices  323 us (49%)
  other arithmetic  103 us (16%)
  matrix products  99.6 us (15%)
  blocking collectives  43 us (7%)
  local copies, waits for them, and re-layouts  41.5 us (6%)
  starting transfers between devices  20.4 us (3%)
  between operations  14.4 us (2%)
    reduce_scatter x1, waiting for transfers between devices, shards(): lax.psum_scatter(w_in_term, ('dp', 'row', 'col'), scatter_dimension=0, ti...  146 us
    reduce_scatter x1, waiting for transfers between devices, shards(): lax.psum_scatter(w_out_term, ('dp', 'row', 'col'), scatter_dimension=0, t...  124 us
    reduce_sum x8, other arithmetic, shards(): dw_terms.append(jnp.sum(g_wide * window, axis=(0, 1, 2)))  82.9 us
    conv_general_dilated x2, matrix products, depthwise(): lax.conv_general_dilated(padded, taps, (1, 1), 'VALID', dimension_numbers...  49.5 us
    psum x1, blocking collectives, shards(): lax.psum((dw_term, gain_contribution, gamma_term), ('dp', 'row', 'col'))  43 us
    psum x1, waiting for transfers between devices, shards(): lax.psum((dw_term, gain_contribution, gamma_term), ('dp', 'row', 'col'))  37.1 us
    ppermute x4, starting transfers between devices, extended(): lax.ppermute(lax.slice_in_dim(block, block.shape[dim] - width, None, axis...  15 us
    ppermute x4, waiting for transfers between devices, extended(): lax.ppermute(lax.slice_in_dim(block, block.shape[dim] - width, None, axis...  13.6 us
  transfers between devices with their start and end apart: 11, of which 6 were waited for; matrix products, arithmetic and copies ran while one was open for 12% of the time, Pallas kernels for 0%

commit v1 on v0

--- a/solution.py
+++ b/solution.py
@@ -91,7 +91,7 @@
     grad_input = (upstream + back).astype(jnp.bfloat16).reshape(images_in.shape)
     images = jnp.float32(batch * lax.axis_size("dp"))
     dw_sum, gain_sum, gamma_sum = lax.psum(
-        (dw_term, gain_contribution, gamma_term), ("dp", "row", "col")
+        lax.psum((dw_term, gain_contribution, gamma_term), ("row", "col")), "dp"
     )
     w_in_term = jnp.dot(normalized_input.T, g_pre, preferred_element_type=jnp.float32)
     w_out_term = jnp.dot(hidden.T, g_branch, preferred_element_type=jnp.float32)

time: 653 us -> 632 us (0.968)
  waiting for transfers between devices: 323 us -> 297 us
    reduce_scatter x1, waiting for transfers between devices: 124 us -> 39.4 us  [shards(): lax.psum_scatter(w_out_term, ('dp', 'row', 'col'), scatter_dimension=0, t...]
    psum x1 -> x2, waiting for transfers between devices: 37.1 us -> 92.7 us  [the longest x1 92.7 us: shards(): lax.psum((dw_term, gain_contribution, gamma_term), ('row', 'col'))]
    psum x1 -> x2, blocking collectives: 43 us -> 45.7 us  [the longest x1 40.5 us: shards(): lax.psum((dw_term, gain_contribution, gamma_term), ('row', 'col'))]
  transfers between devices with their start and end apart: 11 -> 12, of which waited for: 6 -> 6; matrix products, arithmetic and copies ran while one was open for 12% -> 12% of each run, Pallas kernels for 0% -> 0%
where the time goes in v1:
time: 632 us; the launch traced here: 623 us
  waiting for transfers between devices  297 us (47%)
  other arithmetic  103 us (16%)
  matrix products  99.6 us (16%)
  blocking collectives  45.7 us (7%)
  local copies, waits for them, and re-layouts  41.5 us (7%)
  starting transfers between devices  20.1 us (3%)
  between operations  16.2 us (3%)
    reduce_scatter x1, waiting for transfers between devices, shards(): lax.psum_scatter(w_in_term, ('dp', 'row', 'col'), scatter_dimension=0, ti...  147 us
    psum x1, waiting for transfers between devices, shards(): lax.psum((dw_term, gain_contribution, gamma_term), ('row', 'col'))  92.7 us
    reduce_sum x8, other arithmetic, shards(): dw_terms.append(jnp.sum(g_wide * window, axis=(0, 1, 2)))  82.9 us
    conv_general_dilated x2, matrix products, depthwise(): lax.conv_general_dilated(padded, taps, (1, 1), 'VALID', dimension_numbers...  49.5 us
    psum x1, blocking collectives, shards(): lax.psum((dw_term, gain_contribution, gamma_term), ('row', 'col'))  40.5 us
    reduce_scatter x1, waiting for transfers between devices, shards(): lax.psum_scatter(w_out_term, ('dp', 'row', 'col'), scatter_dimension=0, t...  39.4 us
    ppermute x4, waiting for transfers between devices, extended(): lax.ppermute(lax.slice_in_dim(block, block.shape[dim] - width, None, axis...  15.5 us
    ppermute x4, starting transfers between devices, extended(): lax.ppermute(lax.slice_in_dim(block, block.shape[dim] - width, None, axis...  14.6 us
  transfers between devices with their start and end apart: 12, of which 6 were waited for; matrix products, arithmetic and copies ran while one was open for 12% of the time, Pallas kernels for 0%

profile of v1, /device:TPU:0, one launch (start us, length us, event | category | flops | bytes accessed | tf_op | source)
XLA Modules:
  0.0 623.5 jit_solution(16281954076664966088)
XLA Ops:
  8.1 1.3 fusion.121
  9.7 5.0 collective-permute-start
  16.3 6.7 %collective-permute-done = bf16[4,3,16,1024]{3,0,2,1:T(4,128)(2,1)S(1)} collective-permute-done((bf16[4,3,16,1024]{3,0,2,1:T(4,128)(2,1)S(1)}, bf16[4,3,16,1024]{3,0,2,1:T(4,128)(2,1)S(1)}, u32[]{:S(2)}, u32[]{:S(2)}) %collective-permute-start) | collective-permute-done | bytes 393248 | tf_op jit(solution)/shard_map/ppermute | solution.py:17
  23.3 4.3 constant_dynamic-update-slice_fusion.6
  27.9 1.4 copy-done.3
  30.0 1.4 fusion.119
  31.4 2.2 collective-permute-start.2
  34.9 4.2 copy_convert_fusion
  39.9 6.7 %copy.73 = f32[4,16,16,1024]{3,2,1,0:T(8,128)} copy(f32[4,16,16,1024]{3,0,2,1:T(4,128)} %copy_convert_fusion) | data formatting | bytes 8388608 | tf_op jit(solution)/shard_map/convert_element_type | solution.py:62
  47.3 4.4 copy.63
  51.8 25.2 %fusion.122 = (f32[4,16,16]{0,2,1:T(8,128)S(1)}, f32[4,16,16,1024]{3,0,2,1:T(4,128)}) fusion(bf16[7,7,1,1024]{3,2,1,0:T(2,128)(2,1)S(1)} %copy-done.19, bf16[4,22,3,1024]{3,0,2,1:T(4,128)(2,1)S(1)} %collective-permute-done.3, bf16[4,22,16,1024]{3,0,2,1:T(4,128)(2,1)S(1)} %get-tuple-element.115, bf16[4,22,3,1024]{3,0,2,1:T(4,128)(2,1)} %collective-permute-done.2), kind=kOutput, calls=%fused_computation.248 | convolution fusion | flops 115702784 | bytes 8263680 | tf_op jit(solution)/shard_map/conv_general_dilated | solution.py:27
  77.4 6.7 %copy.68 = f32[4,16,16,1024]{3,2,1,0:T(8,128)} copy(f32[4,16,16,1024]{3,0,2,1:T(4,128)} %get-tuple-element.117) | data formatting | bytes 8388608 | tf_op jit(solution)/shard_map/conv_general_dilated | solution.py:27
  84.1 1.4 multiply_reduce_fusion.2
  85.8 2.9 multiply_convert_fusion.2
  89.2 7.0 %multiply_convert_fusion = (bf16[1024,2048]{1,0:T(8,128)(2,1)S(1)}, f32[1024,2048]{1,0:T(8,128)}) fusion(bf16[1024,1024]{1,0:T(8,128)(2,1)S(1)} %multiply_convert_fusion.2, bf16[1024,2048]{1,0:T(8,128)(2,1)S(1)} %copy-done.23), kind=kOutput, calls=%fused_computation.96 | convolution fusion | flops 4305453056 | bytes 18874368 | tf_op jit(solution)/shard_map/dot_general | solution.py:55
  96.3 2.3 copy-done.22
  98.6 6.8 %fusion.59 = (f32[1024]{0:T(1024)S(1)}, bf16[1024,1024]{1,0:T(8,128)(2,1)S(1)}, bf16[1024,1024]{1,0:T(8,128)(2,1)}) fusion(f32[4,16,16,1024]{3,2,1,0:T(8,128)S(1)} %copy-done.11, f32[1024]{0:T(1024)S(1)} %bitcast.150, f32[1024]{0:T(1024)S(1)} %copy-done.24, f32[4,16,16,1024]{3,2,1,0:T(8,128)S(1)} %copy-done.12, ...), kind=kOutput, calls=%fused_computation.154 | convolution fusion | flops 4304403456 | bytes 20983808 | tf_op jit(solution)/shard_map/dot_general | solution.py:58
  105.4 9.9 %fusion.5 = bf16[1024,2048]{1,0:T(8,128)(2,1)S(1)} fusion(f32[1024,2048]{1,0:T(8,128)} %get-tuple-element.119, bf16[1024,1024]{1,0:T(8,128)(2,1)S(1)} %get-tuple-element.98, bf16[2048,1024]{1,0:T(8,128)(2,1)S(1)} %copy-done.22), kind=kOutput, calls=%fused_computation.95 | convolution fusion | flops 4315938816 | bytes 18874368 | tf_op jit(solution)/shard_map/dot_general | solution.py:66
  115.4 5.1 multiply_reduce_fusion
  120.6 1.7 multiply_convert_fusion.1
  123.0 8.2 %fusion.54 = (f32[1024]{0:T(1024)S(1)}, f32[1024]{0:T(1024)S(1)}, f32[1024]{0:T(1024)S(1)}, f32[1024]{0:T(1024)S(1)}, f32[1024]{0:T(1024)S(1)}, /*index=5*/f32[1024]{0:T(1024)S(1)}) fusion(bf16[4,19,16,1024]{3,0,2,1:T(4,128)(2,1)S(1)} %copy-done.4, bf16[4,16,16,1024]{3,2,1,0:T(8,128)(2,1)S(1)} %bitcast.90, bf16[4,19,16,1024]{3,0,2,1:T(4,128)(2,1)S(1)} %copy-done.6), kind=kLoop, calls=%fused_computation.148 | loop fusion | flops 19916800 | bytes 14704640 | tf_op jit(solution)/shard_map/reduce_sum | solution.py:87
  131.2 10.7 %fusion.50 = (f32[1024]{0:T(1024)S(1)}, f32[1024]{0:T(1024)S(1)}, f32[1024]{0:T(1024)S(1)}, f32[1024]{0:T(1024)S(1)}, f32[1024]{0:T(1024)S(1)}, /*index=5*/f32[1024]{0:T(1024)S(1)}) fusion(bf16[4,22,3,1024]{3,0,2,1:T(4,128)(2,1)S(1)} %collective-permute-done.3, bf16[4,22,16,1024]{3,0,2,1:T(4,128)(2,1)S(1)} %copy-done.1, ...), kind=kLoop, calls=%fused_computation.144 | loop fusion | flops 26208256 | bytes 6086656 | tf_op jit(solution)/shard_map/reduce_sum | solution.py:87
  141.9 9.7 %fusion.55 = (f32[1024]{0:T(1024)S(1)}, f32[1024]{0:T(1024)S(1)}, f32[1024]{0:T(1024)S(1)}, f32[1024]{0:T(1024)S(1)}, f32[1024]{0:T(1024)S(1)}, /*index=5*/f32[1024]{0:T(1024)S(1)}) fusion(bf16[4,22,3,1024]{3,0,2,1:T(4,128)(2,1)S(1)} %collective-permute-done.3, bf16[4,22,16,1024]{3,0,2,1:T(4,128)(2,1)S(1)} %copy-done.1, ...), kind=kLoop, calls=%fused_computation.149 | loop fusion | flops 26208256 | bytes 5545984 | tf_op jit(solution)/shard_map/reduce_sum | solution.py:87
  151.6 10.8 %fusion.51 = (f32[1024]{0:T(1024)S(1)}, f32[1024]{0:T(1024)S(1)}, f32[1024]{0:T(1024)S(1)}, f32[1024]{0:T(1024)S(1)}, f32[1024]{0:T(1024)S(1)}, /*index=5*/f32[1024]{0:T(1024)S(1)}) fusion(bf16[4,22,3,1024]{3,0,2,1:T(4,128)(2,1)} %collective-permute-done.2, bf16[4,22,16,1024]{3,0,2,1:T(4,128)(2,1)S(1)} %copy-done.1, bf16[4,16,16,1024]{3,2,1,0:T(8,128)(2,1)S(1)} %bitcast.93), kind=kLoop, calls=%fused_computation.145 | loop fusion | flops 26208256 | bytes 5545984 | tf_op jit(solution)/shard_map/reduce_sum | solution.py:87
  162.4 10.3 %fusion.56 = (f32[1024]{0:T(1024)S(1)}, f32[1024]{0:T(1024)S(1)}, f32[1024]{0:T(1024)S(1)}, f32[1024]{0:T(1024)S(1)}, f32[1024]{0:T(1024)S(1)}, /*index=5*/f32[1024]{0:T(1024)S(1)}) fusion(bf16[4,22,3,1024]{3,0,2,1:T(4,128)(2,1)S(1)} %collective-permute-done.3, bf16[4,22,16,1024]{3,0,2,1:T(4,128)(2,1)S(1)} %copy-done.1, ...), kind=kLoop, calls=%fused_computation.150 | loop fusion | flops 26208256 | bytes 5545984 | tf_op jit(solution)/shard_map/reduce_sum | solution.py:87
  172.7 10.9 %fusion.52 = (f32[1024]{0:T(1024)S(1)}, f32[1024]{0:T(1024)S(1)}, f32[1024]{0:T(1024)S(1)}, f32[1024]{0:T(1024)S(1)}, f32[1024]{0:T(1024)S(1)}, /*index=5*/f32[1024]{0:T(1024)S(1)}) fusion(bf16[4,22,3,1024]{3,0,2,1:T(4,128)(2,1)} %collective-permute-done.2, bf16[4,22,16,1024]{3,0,2,1:T(4,128)(2,1)S(1)} %copy-done.1, bf16[4,16,16,1024]{3,2,1,0:T(8,128)(2,1)S(1)} %bitcast.95), kind=kLoop, calls=%fused_computation.146 | loop fusion | flops 26208256 | bytes 5545984 | tf_op jit(solution)/shard_map/reduce_sum | solution.py:87
  183.6 11.6 %fusion.57 = (f32[1024]{0:T(1024)S(1)}, f32[1024]{0:T(1024)S(1)}, f32[1024]{0:T(1024)S(1)}, f32[1024]{0:T(1024)S(1)}, f32[1024]{0:T(1024)S(1)}, /*index=5*/f32[1024]{0:T(1024)S(1)}, f32[1024]{0:T(1024)S(1)}) fusion(bf16[4,22,3,1024]{3,0,2,1:T(4,128)(2,1)S(1)} %collective-permute-done.3, bf16[4,22,16,1024]{3,0,2,1:T(4,128)(2,1)S(1)} %copy-done.1, ...), kind=kLoop, calls=%fused_computation.151 | loop fusion | flops 29352960 | bytes 7647232 | tf_op jit(solution)/shard_map/reduce_sum | solution.py:87
  195.2 10.8 %fusion.53 = (f32[1024]{0:T(1024)S(1)}, f32[1024]{0:T(1024)S(1)}, f32[1024]{0:T(1024)S(1)}, f32[1024]{0:T(1024)S(1)}, f32[1024]{0:T(1024)S(1)}, /*index=5*/f32[1024]{0:T(1024)S(1)}) fusion(bf16[4,22,16,1024]{3,0,2,1:T(4,128)(2,1)S(1)} %copy-done.1, bf16[4,22,3,1024]{3,0,2,1:T(4,128)(2,1)} %collective-permute-done.2, bf16[4,16,16,1024]{3,2,1,0:T(8,128)(2,1)S(1)} %bitcast.97), kind=kLoop, calls=%fused_computation.147 | loop fusion | flops 26208256 | bytes 5545984 | tf_op jit(solution)/shard_map/reduce_sum | solution.py:87
  206.0 4.6 stack.199
  210.7 92.7 %all-reduce.5.cloned.1.call-done = f32[49,1024]{1,0:T(8,128)} async-done(((f32[49,1024]{1,0:T(8,128)}), f32[49,1024]{1,0:T(8,128)}) %all-reduce.5.cloned.1.call-update) | async-done | bytes 200720 | tf_op jit(solution)/shard_map/psum | solution.py:94
  303.5 10.7 %fusion.124 = f32[2048,1024]{1,0:T(8,128)} fusion(bf16[1024,2048]{1,0:T(8,128)(2,1)} %copy-done.27, bf16[1024,1024]{1,0:T(8,128)(2,1)} %copy-done.28), kind=kOutput, calls=%fused_computation.250 | convolution fusion | flops 4294967296 | bytes 14680064 | tf_op jit(solution)/shard_map/dot_general | solution.py:97
  314.4 10.6 %fusion.123 = f32[1024,2048]{1,0:T(8,128)} fusion(bf16[1024,1024]{1,0:T(8,128)(2,1)} %copy-done.15, bf16[1024,2048]{1,0:T(8,128)(2,1)} %copy-done.26), kind=kOutput, calls=%fused_computation.249 | convolution fusion | flops 4294967296 | bytes 14680064 | tf_op jit(solution)/shard_map/dot_general | solution.py:96
  325.4 5.3 collective-permute-start.4
  331.1 1.3 collective-permute-start.5
  332.4 8.8 %collective-permute-done.4 = bf16[4,3,16,1024]{3,0,2,1:T(4,128)(2,1)S(1)} collective-permute-done((bf16[4,3,16,1024]{3,0,2,1:T(4,128)(2,1)S(1)}, bf16[4,3,16,1024]{3,0,2,1:T(4,128)(2,1)S(1)}, u32[]{:S(2)}, u32[]{:S(2)}) %collective-permute-start.4) | collective-permute-done | bytes 393248 | tf_op jit(solution)/shard_map/ppermute | solution.py:17
  341.3 1.9 constant_dynamic-update-slice_fusion.4
  343.2 3.1 collective-permute-done.5
  346.5 1.6 copy-done.16
  348.5 2.1 collective-permute-start.6
  352.3 40.5 %all-reduce = (f32[1024]{0:T(1024)S(1)}, f32[1024]{0:T(1024)S(1)}) all-reduce(f32[1024]{0:T(1024)S(1)} %get-tuple-element.35, f32[1024]{0:T(1024)S(1)} %get-tuple-element.97), channel_id=1, replica_groups=mesh['dp'=2,'row'=4,'col'=4] {'row','col'}, use_global_device_ids=true, to_apply=%region_58.0 | all-reduce | flops 2048 | bytes 16384 | tf_op jit(solution)/shard_map/psum | solution.py:94
  392.9 5.2 all-reduce.1
  398.7 1.6 broadcast_multiply_fusion.2
  400.3 24.3 %add_convert_fusion = bf16[4,16,16,1024]{3,0,2,1:T(4,128)(2,1)S(1)} fusion(bf16[4,22,3,1024]{3,0,2,1:T(4,128)(2,1)} %collective-permute-done.7, bf16[4,22,16,1024]{3,0,2,1:T(4,128)(2,1)} %copy-done.16, bf16[4,22,3,1024]{3,0,2,1:T(4,128)(2,1)} %collective-permute-done.6, bf16[4,16,16,1024]{3,2,1,0:T(8,128)(2,1)S(1)} %copy-done.14, ...), kind=kOutput, calls=%fused_computation.158 | convolution fusion | flops 117800960 | bytes 8259584 | tf_op jit(solution)/shard_map/conv_general_dilated | solution.py:27
  424.6 1.9 copy.81
  426.5 39.4 %reduce-scatter.5.cloned.1.call-done = f32[64,1024]{1,0:T(8,128)} async-done(((f32[2048,1024]{1,0:T(8,128)}), f32[64,1024]{1,0:T(8,128)}) %reduce-scatter.5.cloned.1.call-update) | async-done | bytes 262160 | tf_op jit(solution)/shard_map/reduce_scatter | solution.py:100
  465.9 1.7 broadcast_multiply_fusion
  467.6 146.6 %reduce-scatter.3.cloned.1.call-done = f32[32,2048]{1,0:T(8,128)} async-done(((f32[1024,2048]{1,0:T(8,128)}), f32[32,2048]{1,0:T(8,128)}) %reduce-scatter.3.cloned.1.call-update) | async-done | bytes 262160 | tf_op jit(solution)/shard_map/reduce_scatter | solution.py:99
  614.2 1.7 broadcast_multiply_fusion.1
  (97 shorter events, 12.0 us)
Async XLA Ops:
  8.0 295.4 %all-reduce.5.cloned.1.call-start = ((), (), s32[]{:S(2)}) async-start(), calls=%async_computation.4 | async-start | bytes 458752 | tf_op jit(solution)/shard_map/psum | solution.py:94
  8.0 15.3 %copy-start.9 = (bf16[4,16,16,1024]{3,2,1,0:T(8,128)(2,1)S(1)}, bf16[4,16,16,1024]{3,2,1,0:T(8,128)(2,1)}, u32[]{:S(2)}) copy-start(bf16[4,16,16,1024]{3,2,1,0:T(8,128)(2,1)} %param.8) | copy-start | bytes 6291460
  9.7 13.3 %collective-permute-start = (bf16[4,3,16,1024]{3,0,2,1:T(4,128)(2,1)S(1)}, bf16[4,3,16,1024]{3,0,2,1:T(4,128)(2,1)S(1)}, u32[]{:S(2)}, u32[]{:S(2)}) collective-permute-start(bf16[4,3,16,1024]{3,0,2,1:T(4,128)(2,1)S(1)} %copy.143), channel_id=1, source_target_pairs={{0,4},{4,8},{8,12},{1,5},{5,9},{9,13},{2,6},{6,10},{10,14},{3,7},{... | collective-permute-start | bytes 1179656 | tf_op jit(solution)/shard_map/ppermute | solution.py:17
  15.0 12.6 %collective-permute-start.1 = (bf16[4,3,16,1024]{3,0,2,1:T(4,128)(2,1)S(1)}, bf16[4,3,16,1024]{3,0,2,1:T(4,128)(2,1)S(1)}, u32[]{:S(2)}, u32[]{:S(2)}) collective-permute-start(bf16[4,3,16,1024]{3,0,2,1:T(4,128)(2,1)S(1)} %copy.144), channel_id=1, source_target_pairs={{4,0},{8,4},{12,8},{5,1},{9,5},{13,9},{6,2},{10,6},{14,10},{7,3},{... | collective-permute-start | bytes 1179656 | tf_op jit(solution)/shard_map/ppermute | solution.py:20
  27.6 2.4 copy-start.5
  27.6 7.3 %copy-start.13 = (bf16[4,16,16,1024]{3,2,1,0:T(8,128)(2,1)S(1)}, bf16[4,16,16,1024]{3,2,1,0:T(8,128)(2,1)}, u32[]{:S(2)}) copy-start(bf16[4,16,16,1024]{3,2,1,0:T(8,128)(2,1)} %param.15) | copy-start | bytes 6291460
  27.9 1.5 copy-start.3
  29.4 22.4 %copy-start = (bf16[4,22,16,1024]{3,0,2,1:T(4,128)(2,1)}, bf16[4,22,16,1024]{3,0,2,1:T(4,128)(2,1)S(1)}, u32[]{:S(2)}) copy-start(bf16[4,22,16,1024]{3,0,2,1:T(4,128)(2,1)S(1)} %get-tuple-element.115) | copy-start | bytes 8650756
  31.4 7.8 %copy-start.17 = (bf16[49,1024]{1,0:T(8,128)(2,1)S(1)}, bf16[49,1024]{1,0:T(8,128)(2,1)}, u32[]{:S(2)}) copy-start(bf16[49,1024]{1,0:T(8,128)(2,1)} %param.10) | copy-start | bytes 301060
  31.4 20.3 %collective-permute-start.2 = (bf16[4,22,3,1024]{3,0,2,1:T(4,128)(2,1)}, bf16[4,22,3,1024]{3,0,2,1:T(4,128)(2,1)}, u32[]{:S(2)}, u32[]{:S(2)}) collective-permute-start(bf16[4,22,3,1024]{3,0,2,1:T(4,128)(2,1)} %get-tuple-element.102), channel_id=1, source_target_pairs={{0,1},{1,2},{2,3},{4,5},{5,6},{6,7},{8,9},{9,10},{10,11},{12,13},{... | collective-permute-start | bytes 1622024 | tf_op jit(solution)/shard_map/ppermute | solution.py:17
  33.6 18.1 %collective-permute-start.3 = (bf16[4,22,3,1024]{3,0,2,1:T(4,128)(2,1)}, bf16[4,22,3,1024]{3,0,2,1:T(4,128)(2,1)S(1)}, u32[]{:S(2)}, u32[]{:S(2)}) collective-permute-start(bf16[4,22,3,1024]{3,0,2,1:T(4,128)(2,1)} %get-tuple-element.103), channel_id=1, source_target_pairs={{1,0},{2,1},{3,2},{5,4},{6,5},{7,6},{9,8},{10,9},{11,10},{13,12},{... | collective-permute-start | bytes 1622024 | tf_op jit(solution)/shard_map/ppermute | solution.py:20
  39.9 6.7 %copy-start.25 = (s32[4]{0:T(128)S(1)}, s32[4]{0:T(128)}, u32[]{:S(2)}) copy-start(s32[4]{0:T(128)} %param.9) | copy-start | bytes 52
  39.9 7.4 %copy-start.7 = (f32[4,16,16,1024]{3,0,2,1:T(4,128)S(1)}, f32[4,16,16,1024]{3,0,2,1:T(4,128)}, u32[]{:S(2)}) copy-start(f32[4,16,16,1024]{3,0,2,1:T(4,128)} %get-tuple-element.105) | copy-start | bytes 12582916
  47.3 4.4 copy-start.19
  77.4 6.7 %copy-start.8 = (f32[4,16,16,1024]{3,0,2,1:T(4,128)S(1)}, f32[4,16,16,1024]{3,0,2,1:T(4,128)}, u32[]{:S(2)}) copy-start(f32[4,16,16,1024]{3,0,2,1:T(4,128)} %get-tuple-element.117) | copy-start | bytes 12582916
  84.1 1.7 copy-start.20
  85.8 3.5 copy-start.23
  89.2 7.0 %copy-start.15 = (bf16[1024,1024]{1,0:T(8,128)(2,1)}, bf16[1024,1024]{1,0:T(8,128)(2,1)S(1)}, u32[]{:S(2)}) copy-start(bf16[1024,1024]{1,0:T(8,128)(2,1)S(1)} %multiply_convert_fusion.2) | copy-start | bytes 6291460
  89.2 7.1 %copy-start.11 = (f32[4,16,16,1024]{3,2,1,0:T(8,128)S(1)}, f32[4,16,16,1024]{3,2,1,0:T(8,128)}, u32[]{:S(2)}) copy-start(f32[4,16,16,1024]{3,2,1,0:T(8,128)} %copy.73) | copy-start | bytes 12582916
  89.2 7.1 %copy-start.12 = (f32[4,16,16,1024]{3,2,1,0:T(8,128)S(1)}, f32[4,16,16,1024]{3,2,1,0:T(8,128)}, u32[]{:S(2)}) copy-start(f32[4,16,16,1024]{3,2,1,0:T(8,128)} %copy.63) | copy-start | bytes 12582916
  89.2 7.1 %copy-start.21 = (f32[1,2,4,128]{3,1,2,0:T(2,128)S(1)}, f32[1,2,4,128]{3,1,2,0:T(2,128)}, u32[]{:S(2)}) copy-start(f32[1,2,4,128]{3,1,2,0:T(2,128)} %copy.82) | copy-start | bytes 12292
  89.2 9.4 %copy-start.22 = (bf16[2048,1024]{1,0:T(8,128)(2,1)S(1)}, bf16[2048,1024]{1,0:T(8,128)(2,1)}, u32[]{:S(2)}) copy-start(bf16[2048,1024]{1,0:T(8,128)(2,1)} %param.13) | copy-start | bytes 12582916
  89.2 9.4 %copy-start.24 = (f32[1024]{0:T(1024)S(1)}, f32[1024]{0:T(1024)}, u32[]{:S(2)}) copy-start(f32[1024]{0:T(1024)} %param.14) | copy-start | bytes 12292
  96.3 9.2 %copy-start.27 = (bf16[1024,2048]{1,0:T(8,128)(2,1)}, bf16[1024,2048]{1,0:T(8,128)(2,1)S(1)}, u32[]{:S(2)}) copy-start(bf16[1024,2048]{1,0:T(8,128)(2,1)S(1)} %get-tuple-element.118) | copy-start | bytes 12582916
  105.4 10.0 %copy-start.28 = (bf16[1024,1024]{1,0:T(8,128)(2,1)}, bf16[1024,1024]{1,0:T(8,128)(2,1)S(1)}, u32[]{:S(2)}) copy-start(bf16[1024,1024]{1,0:T(8,128)(2,1)S(1)} %get-tuple-element.98) | copy-start | bytes 6291460
  105.4 10.0 %copy-start.2 = (f32[4,16,16,1024]{3,2,1,0:T(8,128)S(1)}, f32[4,16,16,1024]{3,2,1,0:T(8,128)}, u32[]{:S(2)}) copy-start(f32[4,16,16,1024]{3,2,1,0:T(8,128)} %copy.68) | copy-start | bytes 12582916
  115.4 5.1 copy-start.26
  120.5 1.7 copy-start.4
  120.5 2.4 copy-start.6
  123.0 8.2 %copy-start.1 = (bf16[4,22,16,1024]{3,0,2,1:T(4,128)(2,1)S(1)}, bf16[4,22,16,1024]{3,0,2,1:T(4,128)(2,1)}, u32[]{:S(2)}) copy-start(bf16[4,22,16,1024]{3,0,2,1:T(4,128)(2,1)} %copy-done) | copy-start | bytes 8650756
  172.7 10.9 %copy-start.10 = (bf16[4,16,16,1024]{3,2,1,0:T(8,128)(2,1)S(1)}, bf16[4,16,16,1024]{3,2,1,0:T(8,128)(2,1)}, u32[]{:S(2)}) copy-start(bf16[4,16,16,1024]{3,2,1,0:T(8,128)(2,1)} %param.8) | copy-start | bytes 6291460
  210.7 188.0 %all-reduce.7.cloned.1.call-start = ((), (), s32[]{:S(2)}) async-start(), calls=%async_computation.5 | async-start | bytes 458752 | tf_op jit(solution)/shard_map/psum | solution.py:93
  303.4 162.5 %reduce-scatter.5.cloned.1.call-start = ((), (), s32[]{:S(2)}) async-start(), calls=%async_computation.3 | async-start | bytes 8650752 | tf_op jit(solution)/shard_map/reduce_scatter | solution.py:100
  314.2 300.0 %reduce-scatter.3.cloned.1.call-start = ((), (), s32[]{:S(2)}) async-start(), calls=%async_computation.2 | async-start | bytes 8650752 | tf_op jit(solution)/shard_map/reduce_scatter | solution.py:99
  325.4 15.7 %collective-permute-start.4 = (bf16[4,3,16,1024]{3,0,2,1:T(4,128)(2,1)S(1)}, bf16[4,3,16,1024]{3,0,2,1:T(4,128)(2,1)S(1)}, u32[]{:S(2)}, u32[]{:S(2)}) collective-permute-start(bf16[4,3,16,1024]{3,0,2,1:T(4,128)(2,1)S(1)} %copy.145), channel_id=1, source_target_pairs={{0,4},{4,8},{8,12},{1,5},{5,9},{9,13},{2,6},{6,10},{10,14},{3,7},{... | collective-permute-start | bytes 1179656 | tf_op jit(solution)/shard_map/ppermute | solution.py:17
  331.1 15.2 %collective-permute-start.5 = (bf16[4,3,16,1024]{3,0,2,1:T(4,128)(2,1)S(1)}, bf16[4,3,16,1024]{3,0,2,1:T(4,128)(2,1)S(1)}, u32[]{:S(2)}, u32[]{:S(2)}) collective-permute-start(bf16[4,3,16,1024]{3,0,2,1:T(4,128)(2,1)S(1)} %copy.146), channel_id=1, source_target_pairs={{4,0},{8,4},{12,8},{5,1},{9,5},{13,9},{6,2},{10,6},{14,10},{7,3},{... | collective-permute-start | bytes 1179656 | tf_op jit(solution)/shard_map/ppermute | solution.py:20
  341.3 10.6 %copy-start.18 = (bf16[49,1024]{1,0:T(8,128)(2,1)S(1)}, bf16[49,1024]{1,0:T(8,128)(2,1)}, u32[]{:S(2)}) copy-start(bf16[49,1024]{1,0:T(8,128)(2,1)} %param.10) | copy-start | bytes 301060
  343.2 57.1 %copy-start.14 = (bf16[4,16,16,1024]{3,2,1,0:T(8,128)(2,1)S(1)}, bf16[4,16,16,1024]{3,2,1,0:T(8,128)(2,1)}, u32[]{:S(2)}) copy-start(bf16[4,16,16,1024]{3,2,1,0:T(8,128)(2,1)} %param.15) | copy-start | bytes 6291460
  346.5 1.6 copy-start.16
  348.5 51.8 %collective-permute-start.6 = (bf16[4,22,3,1024]{3,0,2,1:T(4,128)(2,1)S(1)}, bf16[4,22,3,1024]{3,0,2,1:T(4,128)(2,1)}, u32[]{:S(2)}, u32[]{:S(2)}) collective-permute-start(bf16[4,22,3,1024]{3,0,2,1:T(4,128)(2,1)S(1)} %get-tuple-element.100), channel_id=1, source_target_pairs={{0,1},{1,2},{2,3},{4,5},{5,6},{6,7},{8,9},{9,10},{10,11},{12,13},{... | collective-permute-start | bytes 1622024 | tf_op jit(solution)/shard_map/ppermute | solution.py:17
  350.6 49.7 %collective-permute-start.7 = (bf16[4,22,3,1024]{3,0,2,1:T(4,128)(2,1)S(1)}, bf16[4,22,3,1024]{3,0,2,1:T(4,128)(2,1)}, u32[]{:S(2)}, u32[]{:S(2)}) collective-permute-start(bf16[4,22,3,1024]{3,0,2,1:T(4,128)(2,1)S(1)} %get-tuple-element.101), channel_id=1, source_target_pairs={{1,0},{2,1},{3,2},{5,4},{6,5},{7,6},{9,8},{10,9},{11,10},{13,12},{... | collective-permute-start | bytes 1622024 | tf_op jit(solution)/shard_map/ppermute | solution.py:20
Sparse Core Ops, SparseCore 0:
  210.8 92.5 all-reduce.4
  305.7 26.0 all-reduce.6
Sparse Core Ops, SparseCore 1:
  314.3 151.6 reduce-scatter.4
  468.1 146.0 reduce-scatter.2
